TPU v7x, 256 devices: a whole 4x4x8 slice. The times are simulated.
256 devices in a mesh: turn: 16 (over x, z_lo), tok: 16 (over y, z_hi, core).
Axes of the slice: x: 4, y: 4, z: 8 (z_hi: 2, z_lo: 4; z = z_hi * 4 + z_lo), core: 2. Of those that a mesh axis runs over, the one named last changes fastest.
Arguments:
- activations: bfloat16 [81920, 8192], P(('turn', 'tok')), may hold values from -6 to 6
- output_grads: bfloat16 [81920, 8192], P(('turn', 'tok')), may hold values from -6 to 6
- turn_ids: int32 [81920], P(('turn', 'tok')), may hold values from 0 to 63, as said below
- turn_counts: int32 [64], P('turn'), may hold values from 640 to 3200, as said below
- input_basis: bfloat16 [8192, 256], P('tok'), may hold values from -0.0625 to 0.0625
- output_basis: bfloat16 [8192, 256], P('tok'), may hold values from -0.0625 to 0.0625
- stored_grads: bfloat16 [2048, 65536], P('turn', 'tok'), may hold values from -0.8984375 to 0.8984375
Outputs:
- scores: float32 [64, 2048], P(None, ('turn', 'tok'))
Inputs may be any that keep to these rules, and one draw needn't show every extreme that they name: `turn_ids`: tokens of turn group g (the rows of the devices with turn index g) belong to turns g * 4 to g * 4 + 3 only; within one device the turn ids never fall. turn_counts[t] is the number of tokens s with turn_ids[s] == t; every turn has at least 320 * 16 // 8 tokens.
All inputs are finite; a program needn't handle non-finite values.
Results may differ from a plain program's by a relative error of at most 0.005.
Values may be sent and summed in bfloat16 or wider, within the bound.
A program may use at most 128 MiB of HBM per device.

v0:
```python
import jax
import jax.numpy as jnp
from jax import lax
from jax.sharding import PartitionSpec as P

TURN_G = 4


def local(
    activations, output_grads, turn_ids, turn_counts, input_basis, output_basis, stored_grads
):
    tok_rows = activations.shape[0]
    rank_width = input_basis.shape[1]
    in_sum = jnp.dot(
        activations,
        lax.all_gather(input_basis, "tok", axis=0, tiled=True),
        preferred_element_type=jnp.float32,
    )
    out_sum = jnp.dot(
        output_grads,
        lax.all_gather(output_basis, "tok", axis=0, tiled=True),
        preferred_element_type=jnp.float32,
    )
    in_coords = in_sum.astype(jnp.bfloat16)
    out_coords = out_sum.astype(jnp.bfloat16)
    local_ids = turn_ids - lax.axis_index("turn") * TURN_G
    member = (local_ids[:, None] == jnp.arange(TURN_G, dtype=jnp.int32)[None, :]).astype(
        jnp.bfloat16
    )
    weighted = (member[:, :, None] * in_coords[:, None, :]).reshape(tok_rows, TURN_G * rank_width)
    rank_local = rank_width // lax.axis_size("tok")
    grad_block = lax.psum_scatter(
        lax.dot_general(
            out_coords, weighted, (((0,), (0,)), ((), ())), preferred_element_type=jnp.float32
        ),
        "tok",
        scatter_dimension=0,
        tiled=True,
    )
    counts = turn_counts.astype(jnp.float32)
    scaled = grad_block.reshape(rank_local, TURN_G, rank_width) / counts[None, :, None]
    features = (
        scaled.astype(jnp.bfloat16).transpose(1, 0, 2).reshape(TURN_G, rank_local * rank_width)
    )
    partial_scores = lax.dot_general(
        lax.all_gather(features, "turn", axis=0, tiled=True),
        stored_grads,
        (((1,), (1,)), ((), ())),
        preferred_element_type=jnp.float32,
    )
    return lax.psum_scatter(partial_scores, "tok", scatter_dimension=1, tiled=True)


def solution(mesh):
    placed = (
        P(("turn", "tok"), None),
        P(("turn", "tok"), None),
        P(("turn", "tok")),
        P("turn"),
        P("tok", None),
        P("tok", None),
        P("turn", "tok"),
    )
    return jax.shard_map(
        local, mesh=mesh, in_specs=placed, out_specs=P(None, ("turn", "tok")), check_vma=False
    )
```

profile of v0, /device:TPU:1, one launch (start us, length us, event | category | flops | bytes accessed | tf_op | source)
XLA Modules:
  0.0 379.6 jit_solution(6854849271218336460)
XLA Ops:
  6.5 0.0 copy-start
  6.5 0.0 all-gather.6.cloned.1.call-start
  6.5 0.7 all-gather.6.cloned.1.call-update
  7.3 0.0 all-gather.4.cloned.1.call-start
  7.3 0.7 all-gather.4.cloned.1.call-update
  8.0 0.0 reduce-scatter.2.cloned.1.call-start
  8.1 0.7 broadcast_subtract_fusion
  8.7 0.1 fusion.1
  8.9 82.7 %all-gather.6.cloned.1.call-done = bf16[8192,256]{1,0:T(8,128)(2,1)} async-done(((bf16[512,256]{1,0:T(8,128)(2,1)}), bf16[8192,256]{1,0:T(8,128)(2,1)}) %all-gather.6.cloned.1.call-update) | async-done | bytes 4194320 | tf_op jit(solution)/shard_map/all_gather | solution.py:16
  91.6 5.3 %convolution_convert_fusion = bf16[320,256]{1,0:T(8,128)(2,1)S(1)} fusion(bf16[320,8192]{1,0:T(8,128)(2,1)} %param.7, bf16[8192,256]{1,0:T(8,128)(2,1)} %all-gather.6.cloned.1.call-done), kind=kOutput, calls=%fused_computation | convolution fusion | flops 1342259200 | bytes 9601024 | tf_op jit(solution)/shard_map/dot_general | solution.py:14
  96.9 0.5 broadcast_multiply_fusion
  97.3 0.1 copy.8
  97.5 69.7 %all-gather.4.cloned.1.call-done = bf16[8192,256]{1,0:T(8,128)(2,1)} async-done(((bf16[512,256]{1,0:T(8,128)(2,1)}), bf16[8192,256]{1,0:T(8,128)(2,1)}) %all-gather.4.cloned.1.call-update) | async-done | bytes 4194320 | tf_op jit(solution)/shard_map/all_gather | solution.py:21
  167.1 0.0 copy-start.1
  167.1 0.0 copy-start.2
  167.1 7.3 %fusion = f32[256,1024]{1,0:T(8,128)} fusion(bf16[320,1024]{1,0:T(8,128)(2,1)S(1)} %bitcast.14, bf16[320,8192]{1,0:T(8,128)(2,1)} %param.8, bf16[8192,256]{1,0:T(8,128)(2,1)} %all-gather.4.cloned.1.call-done), kind=kOutput, calls=%fused_computation.2 | convolution fusion | flops 1510031360 | bytes 11141120 | tf_op jit(solution)/shard_map/dot_general | solution.py:33
  174.4 0.0 reduce-scatter.2.cloned.1.call-update
  174.4 0.0 copy-done.1
  174.5 0.0 copy-done.2
  174.5 0.6 dynamic-slice
  175.7 71.7 %reduce-scatter.2.cloned.1.call-done = f32[16,1024]{1,0:T(8,128)} async-done(((f32[256,1024]{1,0:T(8,128)}), f32[16,1024]{1,0:T(8,128)}) %reduce-scatter.2.cloned.1.call-update) | async-done | bytes 65552 | tf_op jit(solution)/shard_map/reduce_scatter | solution.py:32
  247.4 0.9 reshape.34
  248.3 0.1 divide_convert_fusion
  248.3 37.6 %all-gather = bf16[16,4,4096]{2,1,0:T(4,128)(2,1)S(1)} all-gather(bf16[1,4,4096]{2,1,0:T(4,128)(2,1)S(1)} %bitcast.15), channel_id=1, replica_groups=mesh['turn'=16,'tok'=16] {'turn'}, dimensions={0}, use_global_device_ids=true | all-gather | bytes 557056 | tf_op jit(solution)/shard_map/all_gather | solution.py:46
  285.9 0.1 reshape.37
  286.0 0.0 copy-done
  286.0 0.4 fusion.2
  286.5 86.0 %all-reduce = f32[64,128]{0,1:T(8,128)S(1)} all-reduce(f32[64,128]{0,1:T(8,128)S(1)} %fusion.2), channel_id=3, replica_groups=mesh['turn'=16,'tok'=16] {'tok'}, use_global_device_ids=true, to_apply=%region_1.0.clone | all-reduce | flops 8192 | bytes 65536
  372.5 0.6 constant_dynamic-slice_fusion
  (1 shorter events, 0.0 us)
Async XLA Ops:
  6.5 279.5 %copy-start = (bf16[128,4096]{1,0:T(8,128)(2,1)S(1)}, bf16[128,4096]{1,0:T(8,128)(2,1)}, u32[]{:S(2)}) copy-start(bf16[128,4096]{1,0:T(8,128)(2,1)} %param.13) | copy-start | bytes 3145732
  6.5 85.1 %all-gather.6.cloned.1.call-start = ((), (), s32[]{:S(2)}) async-start(), calls=%async_computation.2 | async-start | bytes 4456448 | tf_op jit(solution)/shard_map/all_gather | solution.py:16
  7.3 159.9 %all-gather.4.cloned.1.call-start = ((), (), s32[]{:S(2)}) async-start(), calls=%async_computation.1 | async-start | bytes 4456448 | tf_op jit(solution)/shard_map/all_gather | solution.py:21
  8.0 239.4 %reduce-scatter.2.cloned.1.call-start = ((), (), s32[]{:S(2)}) async-start(), calls=%async_computation.3 | async-start | bytes 1114112 | tf_op jit(solution)/shard_map/reduce_scatter | solution.py:32
  167.1 7.3 %copy-start.1 = (s32[4]{0:T(128)S(1)}, s32[4]{0:T(128)}, u32[]{:S(2)}) copy-start(s32[4]{0:T(128)} %param.10) | copy-start | bytes 52
  167.1 7.3 %copy-start.2 = (u32[256]{0:T(256)S(1)}, u32[256]{0:T(256)}, u32[]{:S(2)}) copy-start(u32[256]{0:T(256)} %constant.13) | copy-start | bytes 3076
Sparse Core Ops, SparseCore 0:
  10.0 81.5 all-gather.5
  94.3 72.8 all-gather.3
  174.5 72.7 reduce-scatter.1
where the time goes:
time: 385 us; the launch traced here: 380 us
  waiting for transfers between devices  225 us (58%)
  blocking collectives  124 us (32%)
  between operations  13.9 us (4%)
  matrix products  12.9 us (3%)
    unnamed x1, blocking collectives  86 us
    all_gather x1, waiting for transfers between devices, local(): lax.all_gather(input_basis, 'tok', axis=0, tiled=True)  82.7 us
    reduce_scatter x1, waiting for transfers between devices, local(): lax.psum_scatter(lax.dot_general(out_coords, weighted, (((0,), (0,)), (()...  71.7 us
    all_gather x1, waiting for transfers between devices, local(): lax.all_gather(output_basis, 'tok', axis=0, tiled=True)  69.7 us
    all_gather x1, blocking collectives, local(): lax.all_gather(features, 'turn', axis=0, tiled=True)  37.6 us
  transfers between devices with their start and end apart: 3, of which 3 were waited for; matrix products, arithmetic and copies ran while one was open for 2% of the time, Pallas kernels for 0%

commit v1 on v0

v1 whole, which is shorter than its diff:
```python
import functools

import jax
import jax.numpy as jnp
from jax import lax
from jax.experimental import pallas as pl
from jax.experimental.pallas import tpu as pltpu
from jax.sharding import PartitionSpec as P

TURN_G = 4
TOK = 320
TOKP = 384
D = 8192
RANK = 256
CH = 512
PC = 256
LAG = 2
EVENTS = 32
BF = jnp.bfloat16
F32 = jnp.float32
MESH = pl.DeviceIdType.MESH


def kernel(
    ids_ref,
    cnt_ref,
    act_hbm,
    og_hbm,
    ib_hbm,
    ob_hbm,
    sg_hbm,
    out_ref,
    A,
    B,
    S,
    acc,
    Gf,
    Gs,
    Hin,
    Pb,
    Rin,
    Fb,
    Ff,
    Sout,
    Q,
    s_act,
    s_own,
    s_sg,
    r_piece,
    s_sib,
    s_x,
    s_yr,
    s_yo,
    s_yz,
    s_zo,
    s_zr,
    s_h,
    r_h,
    s_rs,
    r_rs,
    s_fz,
    s_fx,
    r_f,
    s_q,
    r_q,
):
    T = lax.axis_index("turn")
    K = lax.axis_index("tok")
    x, zl = T // 4, T % 4
    y, h, c = K // 4, (K // 2) % 2, K % 2
    p = x % 2
    z = h * 4 + zl
    edge = (zl == 0) | (zl == 3)

    def tok_of(yy, hh, cc):
        return yy * 4 + hh * 2 + cc

    def zdev(zz):
        return ((x * 4 + zz % 4), tok_of(y, zz // 4, c))

    sib = (T, K + 1 - 2 * c)
    xdev = lambda d: (((x + d + 4) % 4) * 4 + zl, K)
    ydev = lambda d: (T, tok_of((y + d + 4) % 4, h, c))
    zout = zdev(jnp.where(zl == 3, (z + 1) % 8, (z + 7) % 8))
    zin = zdev(jnp.where(zl == 3, (z + 7) % 8, (z + 1) % 8))

    def rcopy(src, dst, ss, rs, dev):
        return pltpu.make_async_remote_copy(
            src_ref=src, dst_ref=dst, send_sem=ss, recv_sem=rs, device_id=dev, device_id_type=MESH
        )

    RB = TOK // 4
    loads = []
    for b, hbm in enumerate((act_hbm, og_hbm)):
        for i in range(4):
            loads.append(
                pltpu.make_async_copy(
                    hbm.at[pl.ds(i * RB, RB)], A.at[b, pl.ds(i * RB, RB)], s_act.at[b * 4 + i]
                )
            )
    own = []
    for b, hbm in enumerate((ib_hbm, ob_hbm)):
        for f in range(2):
            own.append(
                pltpu.make_async_copy(hbm.at[pl.ds(f * PC, PC)], B.at[b, K, f], s_own.at[b * 2 + f])
            )
    stored = pltpu.make_async_copy(sg_hbm, S, s_sg)
    for cp in own:
        cp.start()
    for cp in loads:
        cp.start()
    stored.start()

    barrier = pltpu.get_barrier_semaphore()

    def greet(i, _):
        pl.semaphore_signal(
            barrier, inc=1, device_id=(T, (K + i) % 16), device_id_type=MESH
        )
        pl.semaphore_signal(
            barrier, inc=1, device_id=((T + i) % 16, K), device_id_type=MESH
        )
        return 0

    lax.fori_loop(1, 16, greet, 0)

    @pl.when(edge)
    def _():
        pl.semaphore_signal(barrier, inc=1, device_id=zout, device_id_type=MESH)

    acc[...] = jnp.zeros_like(acc)
    for cp in own:
        cp.wait()

    @pl.when(edge)
    def _():
        pl.semaphore_wait(barrier, 31)

    @pl.when(jnp.logical_not(edge))
    def _():
        pl.semaphore_wait(barrier, 30)

    def piece(b, kk, f):
        return B.at[b, kk, f], r_piece.at[(b * 16 + kk) * 2 + f]

    def send(b, kk, f, sem, dev):
        ref, rs = piece(b, kk, f)
        return rcopy(ref, ref, sem, rs, dev)

    for b in range(2):
        send(b, K, p, s_yo.at[b * 2], ydev(1)).start()
        send(b, K, p, s_yo.at[b * 2 + 1], ydev(-1)).start()

    @pl.when(edge)
    def _():
        for j in range(4):
            f = p if j < 2 else 1 - p
            send(j % 2, K, f, s_zo.at[j], zout).start()

    for j in range(4):
        send(j // 2, K, j % 2, s_sib.at[j], sib).start()
    for cp in loads:
        cp.wait()

    def decode(ev):
        w = jnp.where
        i32 = jnp.int32
        is_own = ev < 4
        is_z = (ev >= 8) & (ev < 12)
        four = (ev < 8) | ((ev >= 12) & (ev < 16)) | ((ev >= 18) & (ev < 22)) | ((ev >= 24) & (ev < 28))
        base = w(ev < 4, 0, w(ev < 8, 4, w(ev < 12, 8, w(ev < 16, 12, w(ev < 18, 16, w(ev < 22, 18, w(ev < 24, 22, w(ev < 28, 24, w(ev < 30, 28, 30)))))))))
        j = ev - base
        other_h = ((ev >= 18) & (ev < 22)) | (ev >= 24)
        near = four & (ev >= 4)
        late = ev >= 28
        from_y = ((ev >= 4) & (ev < 8)) | ((ev >= 16) & (ev < 22)) | ((ev >= 28) & (ev < 30))
        b = w(is_z, j % 2, w(four, j // 2, w(late, 1 - j, j)))
        s = w(four, j % 2, j)
        yy = w(near, (y + 3 + 2 * s) % 4, (y + 2) % 4)
        hh = w(other_h, 1 - h, h)
        kk = w(is_own, K, w(is_z, tok_of(y, 1 - h, c), tok_of(yy, hh, c)))
        f = w(is_own, j % 2, w(is_z, w(j < 2, p, 1 - p), w(from_y, p, 1 - p)))
        relay = (((ev >= 4) & (ev < 8)) & (b == s)) | (((ev >= 18) & (ev < 22)) & (b != s))
        return b, kk, f, s, is_z, from_y, relay, j

    def dots(b, kk, f):
        col = pl.multiple_of(kk * CH + f * PC, PC)
        acc[b, pl.ds(0, TOK)] += jnp.dot(
            A[b, :, pl.ds(col, PC)], B[b, kk, f], preferred_element_type=F32
        )

    def step(ev, _):
        @pl.when(ev < EVENTS)
        def _():
            b, kk, f, s, is_z, from_y, relay, j = decode(ev)

            @pl.when(ev >= 4)
            def _():
                send(b, kk, f, s_sib.at[ev], sib).wait_recv()

            @pl.when(from_y)
            def _():
                d = jnp.where(s == 0, 1, -1)

                @pl.when(relay)
                def _():
                    send(b, kk, f, s_yr.at[ev], ydev(d)).start()

                send(b, kk, f, s_x.at[ev], xdev(d)).start()

            @pl.when(is_z)
            def _():
                @pl.when(edge)
                def _():
                    send(b, kk, f, s_zr.at[j], zin).start()

                @pl.when(j < 2)
                def _():
                    send(b, kk, f, s_yz.at[j * 2], ydev(1)).start()
                    send(b, kk, f, s_yz.at[j * 2 + 1], ydev(-1)).start()

            @pl.when(ev >= 4)
            def _():
                send(b, kk, f, s_sib.at[ev], sib).start()

            dots(b, kk, f)

        @pl.when(ev >= LAG)
        def _():
            b, kk, f, s, is_z, from_y, relay, j = decode(ev - LAG)
            ko = kk + 1 - 2 * c
            send(b, ko, f, s_sib.at[0], sib).wait_recv()
            dots(b, ko, f)

        return 0

    lax.fori_loop(0, EVENTS + LAG, step, 0)

    in_c = acc[0].astype(BF)
    out_t = acc[1].T
    local = ids_ref[...] - T * TURN_G
    for t in range(TURN_G):
        lhs = jnp.where(local == t, out_t, 0.0).astype(BF)
        g = jnp.dot(lhs, in_c, preferred_element_type=F32).reshape(8, 2, 16, RANK)
        for cc in range(2):
            Gf[cc, :, pl.ds(t * 16, 16), :] = g[:, cc]
            Gs[cc, :, pl.ds(t * 16, 16), :] = g[:, cc].astype(BF)
    hc = rcopy(Gs.at[1 - c], Hin, s_h, r_h, sib)
    hc.start()
    hc.wait_recv()
    me = y * 2 + h

    def rs_copy(i, m, slot):
        return rcopy(Pb.at[m], Rin.at[slot], s_rs.at[i], r_rs.at[slot], (T, m * 2 + c))

    def rs_out(i, _):
        m = (me + i) % 8
        Pb[m] = (Gf[c, m] + Hin[m].astype(F32)).astype(BF)
        rs_copy(i, m, me).start()
        return 0

    lax.fori_loop(1, 8, rs_out, 0)
    Gf[c, me] = Gf[c, me] + Hin[me].astype(F32)

    def rs_in(i, _):
        m = (me + 8 - i) % 8
        rs_copy(i, m, m).wait_recv()
        Gf[c, me] = Gf[c, me] + Rin[m].astype(F32)
        return 0

    lax.fori_loop(1, 8, rs_in, 0)
    for t in range(TURN_G):
        n = cnt_ref[t].astype(F32)
        rows = pl.ds(t * 16, 16)
        Fb[T, rows] = (Gf[c, me, rows] / n).astype(BF)

    def fz(i, zz, slot):
        return rcopy(Fb.at[slot], Fb.at[slot], s_fz.at[i], r_f.at[slot], (x * 4 + zz, K))

    def fx(i, q, xx, slot):
        return rcopy(
            Fb.at[slot], Fb.at[slot], s_fx.at[q * 4 + i], r_f.at[slot], (xx * 4 + zl, K)
        )

    def unpack(slot):
        rows = pl.ds(pl.multiple_of(slot * 64, 64), 64)
        for half in range(2):
            Ff[half, rows] = Fb[slot, :, half * 128 : (half + 1) * 128].astype(F32)

    for i in range(1, 4):
        fz(i, (zl + i) % 4, T).start()
    for i in range(1, 4):
        fx(i, 0, (x + i) % 4, T).start()
    unpack(T)

    def hand(q, _):
        zz = (zl + 4 - q) % 4
        slot = x * 4 + zz
        fz(q, zz, slot).wait_recv()
        for i in range(1, 4):
            fx(i, q, (x + i) % 4, slot).start()
        unpack(slot)
        return 0

    lax.fori_loop(1, 4, hand, 0)

    def arrive(n, _):
        q, i = n // 3, n % 3 + 1
        slot = ((x + 4 - i) % 4) * 4 + (zl + 4 - q) % 4
        fx(i, q, (x + i) % 4, slot).wait_recv()
        unpack(slot)
        return 0

    lax.fori_loop(0, 12, arrive, 0)
    stored.wait()
    sc = jnp.zeros((128, 64), F32)
    for a in range(16):
        feat = jnp.concatenate(
            [Ff[half, pl.ds(a, 64, stride=16), :] for half in range(2)], axis=1
        ).astype(BF)
        sc = sc + lax.dot_general(
            S[:, a * RANK : (a + 1) * RANK], feat, (((1,), (1,)), ((), ())), preferred_element_type=F32
        )
    Sout[:, pl.ds(0, 64)] = sc
    Sout[:, pl.ds(64, 64)] = jnp.zeros((128, 64), F32)

    def q_copy(i, k, slot):
        return rcopy(
            Sout.at[pl.ds(pl.multiple_of(k * 8, 8), 8)], Q.at[slot], s_q.at[i], r_q.at[slot], (T, k)
        )

    def q_out(i, _):
        q_copy(i, (K + i) % 16, K).start()
        return 0

    lax.fori_loop(1, 16, q_out, 0)

    def q_in(i, total):
        k = (K + 16 - i) % 16
        q_copy(i, k, k).wait_recv()
        return total + Q[k]

    total = lax.fori_loop(1, 16, q_in, Sout[pl.ds(pl.multiple_of(K * 8, 8), 8), :])
    out_ref[...] = total[:, :64]

    def done(ev, _):
        b, kk, f, s, is_z, from_y, relay, j = decode(ev)
        send(b, kk, f, s_sib.at[ev], sib).wait_send()

        @pl.when(from_y)
        def _():
            send(b, kk, f, s_x.at[ev], sib).wait_send()

        @pl.when(relay)
        def _():
            send(b, kk, f, s_yr.at[ev], sib).wait_send()

        return 0

    lax.fori_loop(0, EVENTS, done, 0)
    for i in range(4):
        send(0, K, 0, s_yo.at[i], sib).wait_send()
        send(0, K, 0, s_yz.at[i], sib).wait_send()

    @pl.when(edge)
    def _():
        for i in range(4):
            send(0, K, 0, s_zo.at[i], zout).wait_send()
            send(0, K, 0, s_zr.at[i], zin).wait_send()

    hc.wait_send()
    lax.fori_loop(1, 8, lambda i, _: (rs_copy(i, me, me).wait_send(), 0)[1], 0)
    for i in range(1, 4):
        fz(i, (zl + i) % 4, T).wait_send()
        for q in range(4):
            fx(i, q, (x + i) % 4, T).wait_send()
    lax.fori_loop(1, 16, lambda i, _: (q_copy(i, K, K).wait_send(), 0)[1], 0)


def local(
    activations, output_grads, turn_ids, turn_counts, input_basis, output_basis, stored_grads
):
    ids = jnp.pad(turn_ids, (0, TOKP - TOK), constant_values=-1).reshape(1, TOKP)
    dma = pltpu.SemaphoreType.DMA
    hbm = pl.BlockSpec(memory_space=pl.ANY)
    out = pl.pallas_call(
        kernel,
        out_shape=jax.ShapeDtypeStruct((8, 64), F32),
        in_specs=[
            pl.BlockSpec(memory_space=pltpu.VMEM),
            pl.BlockSpec(memory_space=pltpu.SMEM),
            hbm,
            hbm,
            hbm,
            hbm,
            hbm,
        ],
        out_specs=pl.BlockSpec(memory_space=pltpu.VMEM),
        scratch_shapes=[
            pltpu.VMEM((2, TOK, D), BF),
            pltpu.VMEM((2, 16, 2, PC, RANK), BF),
            pltpu.VMEM((128, 4096), BF),
            pltpu.VMEM((2, TOKP, RANK), F32),
            pltpu.VMEM((2, 8, 64, RANK), F32),
            pltpu.VMEM((2, 8, 64, RANK), BF),
            pltpu.VMEM((8, 64, RANK), BF),
            pltpu.VMEM((8, 64, RANK), BF),
            pltpu.VMEM((8, 64, RANK), BF),
            pltpu.VMEM((16, 64, RANK), BF),
            pltpu.VMEM((2, 1024, 128), F32),
            pltpu.VMEM((128, 128), F32),
            pltpu.VMEM((16, 8, 128), F32),
            dma((8,)),
            dma((4,)),
            dma,
            dma((64,)),
            dma((EVENTS,)),
            dma((EVENTS,)),
            dma((EVENTS,)),
            dma((4,)),
            dma((4,)),
            dma((4,)),
            dma((4,)),
            dma,
            dma,
            dma((8,)),
            dma((8,)),
            dma((4,)),
            dma((16,)),
            dma((16,)),
            dma((16,)),
            dma((16,)),
        ],
        compiler_params=pltpu.CompilerParams(
            collective_id=0, has_side_effects=True, vmem_limit_bytes=60 * 1024 * 1024
        ),
        cost_estimate=pl.CostEstimate(
            flops=2 * 1460000000, bytes_accessed=12 * 1024 * 1024, transcendentals=0
        ),
    )(
        ids,
        turn_counts,
        activations,
        output_grads,
        input_basis,
        output_basis,
        stored_grads,
    )
    return out.T


def solution(mesh):
    placed = (
        P(("turn", "tok"), None),
        P(("turn", "tok"), None),
        P(("turn", "tok")),
        P("turn"),
        P("tok", None),
        P("tok", None),
        P("turn", "tok"),
    )
    return jax.shard_map(
        local, mesh=mesh, in_specs=placed, out_specs=P(None, ("turn", "tok")), check_vma=False
    )
```

time: 385 us -> 87.8 us (0.23); the launches traced: 380 us -> 87.7 us
  waiting for transfers between devices: 225 us -> 0 us
  blocking collectives: 124 us -> 0 us
  Pallas kernels: 0 us -> 85.1 us
  between operations: 13.9 us -> 0.01 us
  matrix products: 12.9 us -> 0 us
    all_gather x2 -> x0, waiting for transfers between devices: 152 us -> none  [the longest x1 82.7 us: local(): lax.all_gather(input_basis, 'tok', axis=0, tiled=True)]
    unnamed x1 -> x0, blocking collectives: 86 us -> none
    pallas_call x0 -> x1, Pallas kernels: none -> 85.1 us  [local(): pl.pallas_call(kernel, out_shape=jax.ShapeDtypeStruct((8, 64), F32), in_s...]
    reduce_scatter x1 -> x0, waiting for transfers between devices: 71.7 us -> none  [local(): lax.psum_scatter(lax.dot_general(out_coords, weighted, (((0,), (0,)), (()...]
    all_gather x1 -> x0, blocking collectives: 37.6 us -> none  [local(): lax.all_gather(features, 'turn', axis=0, tiled=True)]
    dot_general x3 -> x0, matrix products: 12.9 us -> none  [the longest x1 7.25 us: local(): lax.dot_general(out_coords, weighted, (((0,), (0,)), ((), ())), preferred...]
  transfers between devices with their start and end apart: 3 -> 0, of which waited for: 3 -> 0; matrix products, arithmetic and copies ran while one was open for 2% -> 0% of each run, Pallas kernels for 0% -> 0%
where the time goes in v1:
time: 87.8 us; the launch traced here: 87.7 us
  Pallas kernels  85.1 us (97%)
  local copies, waits for them, and re-layouts  2.53 us (3%)
    pallas_call x1, Pallas kernels, local(): pl.pallas_call(kernel, out_shape=jax.ShapeDtypeStruct((8, 64), F32), in_s...  85.1 us

profile of v1, /device:TPU:1, one launch (start us, length us, event | category | flops | bytes accessed | tf_op | source)
XLA Modules:
  0.0 87.7 jit_solution(10688209781319203404)
XLA Ops:
  0.0 0.7 pad.4
  0.7 0.6 reshape.3.ids_ref
  1.3 85.1 %shard_map.73 = f32[8,64]{1,0:T(8,128)} custom-call(s32[1,384]{1,0:T(1,128)} %reshape.3.ids_ref, s32[4]{0:T(128)} %cnt_ref.1, bf16[320,8192]{1,0:T(8,128)(2,1)} %act_hbm.1, bf16[320,8192]{1,0:T(8,128)(2,1)} %og_hbm.1, bf16[512,256]{1,0:T(8,128)(2,1)} %ib_hbm.1, bf16[512,256]{1,0:T(8,128)(2,1)} %ob_hbm.1, bf16[128,4096]{1,0:T(8,128)(2,1)} %sg_hbm.1), custom_call_target="tpu_custom_call" | custom-call | flops 2920000000 | bytes 12582912 | tf_op jit(solution)/shard_map/pallas_call | solution.py:386
  86.4 1.3 %copy.9 = f32[64,8]{0,1:T(8,128)} copy(f32[64,8]{0,1:T(8,128)} %bitcast.1) | data formatting | bytes 4096

commit v2 on v1

--- a/solution.py
+++ b/solution.py
@@ -14,8 +14,16 @@
 RANK = 256
 CH = 512
 PC = 256
-LAG = 2
-EVENTS = 32
+NS = 2
+ORDER = (
+    8, 24, 9, 25, 4, 40, 56, 10, 26, 41, 57, 5, 11, 27, 12, 42,
+    58, 16, 36, 43, 59, 17, 28, 48, 14, 13, 29, 49, 37, 18, 60, 6,
+    19, 30, 50, 20, 44, 7, 15, 31, 51, 61, 38, 62, 52, 21, 45, 39,
+    22, 46, 53, 63, 54, 23, 47, 55,
+)
+HALVES = ((1, 0, 0), (3, 0, 0), (1, 0, 1), (3, 0, 1), (2, 0, 0), (0, 1, 0), (2, 0, 1), (3, 1, 0), (1, 1, 0), (0, 1, 1), (2, 1, 0), (3, 1, 1), (1, 1, 1), (2, 1, 1))
+SEND_MAX = 4 * NS + 4 * NS + len(ORDER) * 2
+LAG = 2 * NS
 BF = jnp.bfloat16
 F32 = jnp.float32
 MESH = pl.DeviceIdType.MESH
@@ -34,6 +42,7 @@
     B,
     S,
     acc,
+    ids,
     Gf,
     Gs,
     Hin,
@@ -47,13 +56,10 @@
     s_own,
     s_sg,
     r_piece,
+    r_sib,
     s_sib,
-    s_x,
-    s_yr,
-    s_yo,
-    s_yz,
-    s_zo,
-    s_zr,
+    s_fwd,
+    s_out,
     s_h,
     r_h,
     s_rs,
@@ -68,10 +74,10 @@
     K = lax.axis_index("tok")
     x, zl = T // 4, T % 4
     y, h, c = K // 4, (K // 2) % 2, K % 2
-    p = x % 2
     z = h * 4 + zl
     edge = (zl == 0) | (zl == 3)
-
+    inner = ((zl + 1) // 2) % 2
+    p = (x + inner) % 2
     def tok_of(yy, hh, cc):
         return yy * 4 + hh * 2 + cc
 
@@ -81,8 +87,10 @@
     sib = (T, K + 1 - 2 * c)
     xdev = lambda d: (((x + d + 4) % 4) * 4 + zl, K)
     ydev = lambda d: (T, tok_of((y + d + 4) % 4, h, c))
-    zout = zdev(jnp.where(zl == 3, (z + 1) % 8, (z + 7) % 8))
-    zin = zdev(jnp.where(zl == 3, (z + 7) % 8, (z + 1) % 8))
+    pair = (x * 4 + zl + 1 - 2 * (zl % 2), K)
+    up = jnp.where(zl >= 2, 1, 7)
+    over1 = zdev((z + up) % 8)
+    over2 = zdev((z + up * 2) % 8)
 
     def rcopy(src, dst, ss, rs, dev):
         return pltpu.make_async_remote_copy(
@@ -90,6 +98,7 @@
         )
 
     RB = TOK // 4
+    R = PC // NS
     loads = []
     for b, hbm in enumerate((act_hbm, og_hbm)):
         for i in range(4):
@@ -124,121 +133,149 @@
 
     lax.fori_loop(1, 16, greet, 0)
 
+    pl.semaphore_signal(barrier, inc=1, device_id=over2, device_id_type=MESH)
+
     @pl.when(edge)
     def _():
-        pl.semaphore_signal(barrier, inc=1, device_id=zout, device_id_type=MESH)
+        pl.semaphore_signal(barrier, inc=1, device_id=over1, device_id_type=MESH)
 
     acc[...] = jnp.zeros_like(acc)
+    ids[...] = jnp.full_like(ids, -1)
+    ids[:, pl.ds(0, TOK)] = ids_ref[...]
     for cp in own:
         cp.wait()
 
     @pl.when(edge)
     def _():
-        pl.semaphore_wait(barrier, 31)
+        pl.semaphore_wait(barrier, 32)
 
     @pl.when(jnp.logical_not(edge))
     def _():
-        pl.semaphore_wait(barrier, 30)
-
-    def piece(b, kk, f):
-        return B.at[b, kk, f], r_piece.at[(b * 16 + kk) * 2 + f]
-
-    def send(b, kk, f, sem, dev):
-        ref, rs = piece(b, kk, f)
-        return rcopy(ref, ref, sem, rs, dev)
+        pl.semaphore_wait(barrier, 31)
+
+    def part(b, kk, f, i):
+        return B.at[b, kk, f, pl.ds(i * R, R)], r_piece.at[((b * 16 + kk) * 2 + f) * NS + i]
+
+    sent = []
+
+    def send(b, kk, f, i, dev):
+        ref, rs = part(b, kk, f, i)
+        cp = rcopy(ref, ref, s_fwd.at[len(sent)], rs, dev)
+        cp.start()
+        sent.append(cp)
 
     for b in range(2):
-        send(b, K, p, s_yo.at[b * 2], ydev(1)).start()
-        send(b, K, p, s_yo.at[b * 2 + 1], ydev(-1)).start()
+        for i in range(NS):
+            send(b, K, p, i, ydev(1))
+            send(b, K, p, i, ydev(-1))
+
+    def boundary():
+        out = []
+        for b in range(2):
+            for i in range(NS):
+                for far, (dev, f) in enumerate(((over1, p), (over2, 1 - p))):
+                    ref, rs = part(b, K, f, i)
+                    out.append(rcopy(ref, ref, s_out.at[(b * NS + i) * 2 + far], rs, dev))
+        return out
 
     @pl.when(edge)
     def _():
-        for j in range(4):
-            f = p if j < 2 else 1 - p
-            send(j % 2, K, f, s_zo.at[j], zout).start()
-
-    for j in range(4):
-        send(j // 2, K, j % 2, s_sib.at[j], sib).start()
-    for cp in loads:
-        cp.wait()
-
-    def decode(ev):
-        w = jnp.where
-        i32 = jnp.int32
-        is_own = ev < 4
-        is_z = (ev >= 8) & (ev < 12)
-        four = (ev < 8) | ((ev >= 12) & (ev < 16)) | ((ev >= 18) & (ev < 22)) | ((ev >= 24) & (ev < 28))
-        base = w(ev < 4, 0, w(ev < 8, 4, w(ev < 12, 8, w(ev < 16, 12, w(ev < 18, 16, w(ev < 22, 18, w(ev < 24, 22, w(ev < 28, 24, w(ev < 30, 28, 30)))))))))
-        j = ev - base
-        other_h = ((ev >= 18) & (ev < 22)) | (ev >= 24)
-        near = four & (ev >= 4)
-        late = ev >= 28
-        from_y = ((ev >= 4) & (ev < 8)) | ((ev >= 16) & (ev < 22)) | ((ev >= 28) & (ev < 30))
-        b = w(is_z, j % 2, w(four, j // 2, w(late, 1 - j, j)))
-        s = w(four, j % 2, j)
-        yy = w(near, (y + 3 + 2 * s) % 4, (y + 2) % 4)
-        hh = w(other_h, 1 - h, h)
-        kk = w(is_own, K, w(is_z, tok_of(y, 1 - h, c), tok_of(yy, hh, c)))
-        f = w(is_own, j % 2, w(is_z, w(j < 2, p, 1 - p), w(from_y, p, 1 - p)))
-        relay = (((ev >= 4) & (ev < 8)) & (b == s)) | (((ev >= 18) & (ev < 22)) & (b != s))
-        return b, kk, f, s, is_z, from_y, relay, j
-
-    def dots(b, kk, f):
-        col = pl.multiple_of(kk * CH + f * PC, PC)
+        for cp in boundary():
+            cp.start()
+
+    shared = []
+
+    def share(b, kk, f):
+        ref = B.at[b, kk] if f is None else B.at[b, kk, f]
+        rs = r_sib.at[(b * 16 + kk) * 2 + (0 if f is None else f)]
+        cp = rcopy(ref, ref, s_sib.at[len(shared)], rs, sib)
+        cp.start()
+        shared.append(cp)
+
+    def share_wait(b, kk, f):
+        ref = B.at[b, kk] if f is None else B.at[b, kk, f]
+        rs = r_sib.at[(b * 16 + kk) * 2 + (0 if f is None else f)]
+        rcopy(ref, ref, s_sib.at[0], rs, sib).wait_recv()
+
+    for b in range(2):
+        share(b, K, None)
+    KO = K + 1 - 2 * c
+
+    def place(dy, dh, half):
+        hh = h if dh == 0 else 1 - h
+        return tok_of((y + dy) % 4, hh, c), (p if half == 0 else 1 - p)
+
+    def dots(b, blocks):
+        lhs, rhs = [], []
+        for kk, f in blocks:
+            col = pl.multiple_of(kk * CH + f * PC, PC)
+            lhs.append(A[b, :, pl.ds(col, PC)])
+            rhs.append(B[b, kk, f])
         acc[b, pl.ds(0, TOK)] += jnp.dot(
-            A[b, :, pl.ds(col, PC)], B[b, kk, f], preferred_element_type=F32
-        )
-
-    def step(ev, _):
-        @pl.when(ev < EVENTS)
-        def _():
-            b, kk, f, s, is_z, from_y, relay, j = decode(ev)
-
-            @pl.when(ev >= 4)
-            def _():
-                send(b, kk, f, s_sib.at[ev], sib).wait_recv()
-
-            @pl.when(from_y)
-            def _():
-                d = jnp.where(s == 0, 1, -1)
-
-                @pl.when(relay)
-                def _():
-                    send(b, kk, f, s_yr.at[ev], ydev(d)).start()
-
-                send(b, kk, f, s_x.at[ev], xdev(d)).start()
-
-            @pl.when(is_z)
-            def _():
-                @pl.when(edge)
-                def _():
-                    send(b, kk, f, s_zr.at[j], zin).start()
-
-                @pl.when(j < 2)
-                def _():
-                    send(b, kk, f, s_yz.at[j * 2], ydev(1)).start()
-                    send(b, kk, f, s_yz.at[j * 2 + 1], ydev(-1)).start()
-
-            @pl.when(ev >= 4)
-            def _():
-                send(b, kk, f, s_sib.at[ev], sib).start()
-
-            dots(b, kk, f)
-
-        @pl.when(ev >= LAG)
-        def _():
-            b, kk, f, s, is_z, from_y, relay, j = decode(ev - LAG)
+            jnp.concatenate(lhs, axis=1), jnp.concatenate(rhs, axis=0), preferred_element_type=F32
+        )
+
+    def dots_of(b, group):
+        if group == 0:
+            if b == 0:
+                for cp in loads[:4]:
+                    cp.wait()
+            else:
+                for cp in loads[4:]:
+                    cp.wait()
+            share_wait(b, KO, None)
+            dots(b, [(K, 0), (K, 1), (KO, 0), (KO, 1)])
+            return
+        blocks = []
+        for q in HALVES[2 * group - 2 : 2 * group]:
+            kk, f = place(*q)
             ko = kk + 1 - 2 * c
-            send(b, ko, f, s_sib.at[0], sib).wait_recv()
-            dots(b, ko, f)
-
-        return 0
-
-    lax.fori_loop(0, EVENTS + LAG, step, 0)
+            share_wait(b, ko, f)
+            blocks += [(kk, f), (ko, f)]
+        dots(b, blocks)
+
+    seen = [{}, {}]
+    for n, code in enumerate(ORDER):
+        i, half, dh, dy, b = code % NS, code // NS % 2, code // NS // 2 % 2, code // NS // 4 % 4, code // NS // 16
+        seen[b][(dy, dh, half)] = n
+    due = []
+    for b in range(2):
+        due.append((NS + NS * b, b, 0))
+        for group in range(1, 8):
+            last = max(seen[b][q] for q in HALVES[2 * group - 2 : 2 * group])
+            due.append((last + LAG, b, group))
+    due.sort(key=lambda e: (e[0], e[2]))
+
+    parts = {}
+    for n, code in enumerate(ORDER):
+        i, half, dh, dy, b = code % NS, code // NS % 2, code // NS // 2 % 2, code // NS // 4 % 4, code // NS // 16
+        kk, f = place(dy, dh, half)
+        ref, rs = part(b, kk, f, i)
+        rcopy(ref, ref, s_fwd.at[0], rs, sib).wait_recv()
+        if dy == 0:
+            if half == 0:
+                send(b, kk, f, i, ydev(1))
+                send(b, kk, f, i, ydev(-1))
+                send(b, kk, f, i, pair)
+        elif half == 0:
+            side = {3: 0, 1: 1, 2: b if dh == 0 else 1 - b}[dy]
+            d = 1 if side == 0 else -1
+            if dy != 2 and (b == side) == (dh == 0):
+                send(b, kk, f, i, ydev(d))
+            send(b, kk, f, i, xdev(d))
+        got = parts.setdefault((b, dy, dh, half), set())
+        got.add(i)
+        if len(got) == NS:
+            share(b, kk, f)
+        while due and due[0][0] <= n:
+            _, bb, group = due.pop(0)
+            dots_of(bb, group)
+    for _, bb, group in due:
+        dots_of(bb, group)
 
     in_c = acc[0].astype(BF)
     out_t = acc[1].T
-    local = ids_ref[...] - T * TURN_G
+    local = ids[...] - T * TURN_G
     for t in range(TURN_G):
         lhs = jnp.where(local == t, out_t, 0.0).astype(BF)
         g = jnp.dot(lhs, in_c, preferred_element_type=F32).reshape(8, 2, 16, RANK)
@@ -260,6 +297,14 @@
         return 0
 
     lax.fori_loop(1, 8, rs_out, 0)
+    for cp in sent + shared:
+        cp.wait_send()
+
+    @pl.when(edge)
+    def _():
+        for cp in boundary():
+            cp.wait_send()
+
     Gf[c, me] = Gf[c, me] + Hin[me].astype(F32)
 
     def rs_in(i, _):
@@ -343,31 +388,6 @@
     total = lax.fori_loop(1, 16, q_in, Sout[pl.ds(pl.multiple_of(K * 8, 8), 8), :])
     out_ref[...] = total[:, :64]
 
-    def done(ev, _):
-        b, kk, f, s, is_z, from_y, relay, j = decode(ev)
-        send(b, kk, f, s_sib.at[ev], sib).wait_send()
-
-        @pl.when(from_y)
-        def _():
-            send(b, kk, f, s_x.at[ev], sib).wait_send()
-
-        @pl.when(relay)
-        def _():
-            send(b, kk, f, s_yr.at[ev], sib).wait_send()
-
-        return 0
-
-    lax.fori_loop(0, EVENTS, done, 0)
-    for i in range(4):
-        send(0, K, 0, s_yo.at[i], sib).wait_send()
-        send(0, K, 0, s_yz.at[i], sib).wait_send()
-
-    @pl.when(edge)
-    def _():
-        for i in range(4):
-            send(0, K, 0, s_zo.at[i], zout).wait_send()
-            send(0, K, 0, s_zr.at[i], zin).wait_send()
-
     hc.wait_send()
     lax.fori_loop(1, 8, lambda i, _: (rs_copy(i, me, me).wait_send(), 0)[1], 0)
     for i in range(1, 4):
@@ -380,7 +400,7 @@
 def local(
     activations, output_grads, turn_ids, turn_counts, input_basis, output_basis, stored_grads
 ):
-    ids = jnp.pad(turn_ids, (0, TOKP - TOK), constant_values=-1).reshape(1, TOKP)
+    ids = turn_ids.reshape(1, TOK)
     dma = pltpu.SemaphoreType.DMA
     hbm = pl.BlockSpec(memory_space=pl.ANY)
     out = pl.pallas_call(
@@ -401,6 +421,7 @@
             pltpu.VMEM((2, 16, 2, PC, RANK), BF),
             pltpu.VMEM((128, 4096), BF),
             pltpu.VMEM((2, TOKP, RANK), F32),
+            pltpu.VMEM((1, TOKP), jnp.int32),
             pltpu.VMEM((2, 8, 64, RANK), F32),
             pltpu.VMEM((2, 8, 64, RANK), BF),
             pltpu.VMEM((8, 64, RANK), BF),
@@ -413,14 +434,11 @@
             dma((8,)),
             dma((4,)),
             dma,
+            dma((64 * NS,)),
             dma((64,)),
-            dma((EVENTS,)),
-            dma((EVENTS,)),
-            dma((EVENTS,)),
-            dma((4,)),
-            dma((4,)),
-            dma((4,)),
-            dma((4,)),
+            dma((32,)),
+            dma((SEND_MAX,)),
+            dma((4 * NS,)),
             dma,
             dma,
             dma((8,)),

time: 87.8 us -> 76.8 us (0.87)
  Pallas kernels: 85.1 us -> 74.1 us
    pallas_call x1, Pallas kernels: 85.1 us -> 74.1 us  [local(): pl.pallas_call(kernel, out_shape=jax.ShapeDtypeStruct((8, 64), F32), in_s...]
where the time goes in v2:
time: 76.8 us; the launch traced here: 76.6 us
  Pallas kernels  74.1 us (96%)
  local copies, waits for them, and re-layouts  2.52 us (3%)
    pallas_call x1, Pallas kernels, local(): pl.pallas_call(kernel, out_shape=jax.ShapeDtypeStruct((8, 64), F32), in_s...  74.1 us

profile of v2, /device:TPU:1, one launch (start us, length us, event | category | flops | bytes accessed | tf_op | source)
XLA Modules:
  0.0 76.6 jit_solution(3447962660219375864)
XLA Ops:
  0.0 1.2 %reshape.3.ids_ref = s32[1,320]{1,0:T(1,128)} reshape(s32[320]{0:T(512)} %param.9) | data formatting | bytes 2560 | tf_op jit(solution)/shard_map/reshape | solution.py:403
  1.2 74.1 %shard_map.73 = f32[8,64]{1,0:T(8,128)} custom-call(s32[1,320]{1,0:T(1,128)} %reshape.3.ids_ref, s32[4]{0:T(128)} %cnt_ref.1, bf16[320,8192]{1,0:T(8,128)(2,1)} %act_hbm.1, bf16[320,8192]{1,0:T(8,128)(2,1)} %og_hbm.1, bf16[512,256]{1,0:T(8,128)(2,1)} %ib_hbm.1, bf16[512,256]{1,0:T(8,128)(2,1)} %ob_hbm.1, bf16[128,4096]{1,0:T(8,128)(2,1)} %sg_hbm.1), custom_call_target="tpu_custom_call" | custom-call | flops 2920000000 | bytes 12582912 | tf_op jit(solution)/shard_map/pallas_call | solution.py:406
  75.3 1.3 %copy.9 = f32[64,8]{0,1:T(8,128)} copy(f32[64,8]{0,1:T(8,128)} %bitcast.1) | data formatting | bytes 4096

commit v3 on v2

--- a/solution.py
+++ b/solution.py
@@ -16,14 +16,14 @@
 PC = 256
 NS = 2
 ORDER = (
-    8, 24, 9, 25, 4, 40, 56, 10, 26, 41, 57, 5, 11, 27, 12, 42,
-    58, 16, 36, 43, 59, 17, 28, 48, 14, 13, 29, 49, 37, 18, 60, 6,
-    19, 30, 50, 20, 44, 7, 15, 31, 51, 61, 38, 62, 52, 21, 45, 39,
-    22, 46, 53, 63, 54, 23, 47, 55,
+    8, 24, 9, 25, 4, 40, 56, 5, 10, 41, 57, 16, 12, 17, 26, 48,
+    36, 28, 13, 37, 14, 49, 29, 60, 20, 61, 44, 50, 21, 27, 43, 52,
+    45, 53, 58, 46, 63, 15, 23, 6, 62, 19, 39, 42, 22, 54, 7, 38,
+    11, 30, 51, 59, 31, 18, 47, 55,
 )
-HALVES = ((1, 0, 0), (3, 0, 0), (1, 0, 1), (3, 0, 1), (2, 0, 0), (0, 1, 0), (2, 0, 1), (3, 1, 0), (1, 1, 0), (0, 1, 1), (2, 1, 0), (3, 1, 1), (1, 1, 1), (2, 1, 1))
+HALVES = ((1, 0, 0), (3, 0, 0), (0, 1, 0), (2, 0, 0), (3, 1, 0), (1, 1, 0), (2, 1, 0), (0, 1, 1), (1, 0, 1), (3, 0, 1), (3, 1, 1), (2, 0, 1), (1, 1, 1), (2, 1, 1))
 SEND_MAX = 4 * NS + 4 * NS + len(ORDER) * 2
-LAG = 2 * NS
+LAG = 3
 BF = jnp.bfloat16
 F32 = jnp.float32
 MESH = pl.DeviceIdType.MESH
@@ -43,6 +43,7 @@
     S,
     acc,
     ids,
+    OT,
     Gf,
     Gs,
     Hin,
@@ -51,6 +52,8 @@
     Fb,
     Ff,
     Sout,
+    Qh,
+    Sc,
     Q,
     s_act,
     s_own,
@@ -67,6 +70,8 @@
     s_fz,
     s_fx,
     r_f,
+    s_qh,
+    r_qh,
     s_q,
     r_q,
 ):
@@ -141,7 +146,8 @@
 
     acc[...] = jnp.zeros_like(acc)
     ids[...] = jnp.full_like(ids, -1)
-    ids[:, pl.ds(0, TOK)] = ids_ref[...]
+    ids[0, pl.ds(0, TOK)] = ids_ref[...]
+    Sout[...] = jnp.zeros_like(Sout)
     for cp in own:
         cp.wait()
 
@@ -226,13 +232,14 @@
             share_wait(b, KO, None)
             dots(b, [(K, 0), (K, 1), (KO, 0), (KO, 1)])
             return
-        blocks = []
-        for q in HALVES[2 * group - 2 : 2 * group]:
-            kk, f = place(*q)
-            ko = kk + 1 - 2 * c
+        blocks = [place(*q) for q in HALVES[2 * group - 2 : 2 * group]]
+        others = [(kk + 1 - 2 * c, f) for kk, f in blocks]
+        if group == 7:
+            dots(b, blocks)
+            blocks = []
+        for ko, f in others:
             share_wait(b, ko, f)
-            blocks += [(kk, f), (ko, f)]
-        dots(b, blocks)
+        dots(b, blocks + others)
 
     seen = [{}, {}]
     for n, code in enumerate(ORDER):
@@ -274,29 +281,40 @@
         dots_of(bb, group)
 
     in_c = acc[0].astype(BF)
-    out_t = acc[1].T
+    out_t = acc[1].T.reshape(8, 2, 16, TOKP)
+    for cc in range(2):
+        OT[cc] = out_t[:, cc].reshape(128, TOKP)
     local = ids[...] - T * TURN_G
+
+    def gradient(cc, t):
+        lhs = jnp.where(local == t, OT[cc], 0.0).astype(BF)
+        return jnp.dot(lhs, in_c, preferred_element_type=F32).reshape(8, 16, RANK)
+
     for t in range(TURN_G):
-        lhs = jnp.where(local == t, out_t, 0.0).astype(BF)
-        g = jnp.dot(lhs, in_c, preferred_element_type=F32).reshape(8, 2, 16, RANK)
-        for cc in range(2):
-            Gf[cc, :, pl.ds(t * 16, 16), :] = g[:, cc]
-            Gs[cc, :, pl.ds(t * 16, 16), :] = g[:, cc].astype(BF)
-    hc = rcopy(Gs.at[1 - c], Hin, s_h, r_h, sib)
+        Gs[:, pl.ds(t * 16, 16), :] = gradient(1 - c, t).astype(BF)
+    hc = rcopy(Gs, Hin, s_h, r_h, sib)
     hc.start()
+    for t in range(TURN_G):
+        Gf[:, pl.ds(t * 16, 16), :] = gradient(c, t)
     hc.wait_recv()
     me = y * 2 + h
 
+    def peer(i, sign):
+        far = i < 4
+        yy = (y + 4 + sign * jnp.where(far, i, i - 3)) % 4
+        return yy * 2 + jnp.where(far, 1 - h, h)
+
     def rs_copy(i, m, slot):
         return rcopy(Pb.at[m], Rin.at[slot], s_rs.at[i], r_rs.at[slot], (T, m * 2 + c))
 
     def rs_out(i, _):
-        m = (me + i) % 8
-        Pb[m] = (Gf[c, m] + Hin[m].astype(F32)).astype(BF)
+        m = peer(i, 1)
+        Pb[m] = (Gf[m] + Hin[m].astype(F32)).astype(BF)
         rs_copy(i, m, me).start()
         return 0
 
-    lax.fori_loop(1, 8, rs_out, 0)
+    lax.fori_loop(0, 7, rs_out, 0)
+    Gf[me] = Gf[me] + Hin[me].astype(F32)
     for cp in sent + shared:
         cp.wait_send()
 
@@ -305,19 +323,19 @@
         for cp in boundary():
             cp.wait_send()
 
-    Gf[c, me] = Gf[c, me] + Hin[me].astype(F32)
+    hc.wait_send()
 
     def rs_in(i, _):
-        m = (me + 8 - i) % 8
-        rs_copy(i, m, m).wait_recv()
-        Gf[c, me] = Gf[c, me] + Rin[m].astype(F32)
+        m = peer(6 - i, -1)
+        rs_copy(0, m, m).wait_recv()
+        Gf[me] = Gf[me] + Rin[m].astype(F32)
         return 0
 
-    lax.fori_loop(1, 8, rs_in, 0)
+    lax.fori_loop(0, 7, rs_in, 0)
     for t in range(TURN_G):
         n = cnt_ref[t].astype(F32)
         rows = pl.ds(t * 16, 16)
-        Fb[T, rows] = (Gf[c, me, rows] / n).astype(BF)
+        Fb[T, rows] = (Gf[me, rows] / n).astype(BF)
 
     def fz(i, zz, slot):
         return rcopy(Fb.at[slot], Fb.at[slot], s_fz.at[i], r_f.at[slot], (x * 4 + zz, K))
@@ -337,6 +355,7 @@
     for i in range(1, 4):
         fx(i, 0, (x + i) % 4, T).start()
     unpack(T)
+    lax.fori_loop(0, 7, lambda i, _: (rs_copy(i, me, me).wait_send(), 0)[1], 0)
 
     def hand(q, _):
         zz = (zl + 4 - q) % 4
@@ -366,41 +385,41 @@
         sc = sc + lax.dot_general(
             S[:, a * RANK : (a + 1) * RANK], feat, (((1,), (1,)), ((), ())), preferred_element_type=F32
         )
-    Sout[:, pl.ds(0, 64)] = sc
-    Sout[:, pl.ds(64, 64)] = jnp.zeros((128, 64), F32)
-
-    def q_copy(i, k, slot):
-        return rcopy(
-            Sout.at[pl.ds(pl.multiple_of(k * 8, 8), 8)], Q.at[slot], s_q.at[i], r_q.at[slot], (T, k)
-        )
-
-    def q_out(i, _):
-        q_copy(i, (K + i) % 16, K).start()
-        return 0
-
-    lax.fori_loop(1, 16, q_out, 0)
-
-    def q_in(i, total):
-        k = (K + 16 - i) % 16
-        q_copy(i, k, k).wait_recv()
-        return total + Q[k]
-
-    total = lax.fori_loop(1, 16, q_in, Sout[pl.ds(pl.multiple_of(K * 8, 8), 8), :])
-    out_ref[...] = total[:, :64]
-
-    hc.wait_send()
-    lax.fori_loop(1, 8, lambda i, _: (rs_copy(i, me, me).wait_send(), 0)[1], 0)
+    rows = sc.reshape(8, 2, 8, 64)
+    for cc in range(2):
+        Sout[cc, :, :, pl.ds(0, 64)] = rows[:, cc]
+    qh = rcopy(Sout.at[1 - c], Qh, s_qh, r_qh, sib)
+    qh.start()
     for i in range(1, 4):
         fz(i, (zl + i) % 4, T).wait_send()
         for q in range(4):
             fx(i, q, (x + i) % 4, T).wait_send()
-    lax.fori_loop(1, 16, lambda i, _: (q_copy(i, K, K).wait_send(), 0)[1], 0)
+    qh.wait_recv()
+    Sc[...] = Sout[c] + Qh[...]
+
+    def q_copy(i, m, slot):
+        return rcopy(Sc.at[m], Q.at[slot], s_q.at[i], r_q.at[slot], (T, m * 2 + c))
+
+    def q_out(i, _):
+        q_copy(i, peer(i, 1), me).start()
+        return 0
+
+    lax.fori_loop(0, 7, q_out, 0)
+    qh.wait_send()
+
+    def q_in(i, total):
+        m = peer(6 - i, -1)
+        q_copy(0, m, m).wait_recv()
+        return total + Q[m]
+
+    total = lax.fori_loop(0, 7, q_in, Sc[me])
+    out_ref[...] = total[:, :64]
+    lax.fori_loop(0, 7, lambda i, _: (q_copy(i, me, me).wait_send(), 0)[1], 0)
 
 
 def local(
     activations, output_grads, turn_ids, turn_counts, input_basis, output_basis, stored_grads
 ):
-    ids = turn_ids.reshape(1, TOK)
     dma = pltpu.SemaphoreType.DMA
     hbm = pl.BlockSpec(memory_space=pl.ANY)
     out = pl.pallas_call(
@@ -422,15 +441,18 @@
             pltpu.VMEM((128, 4096), BF),
             pltpu.VMEM((2, TOKP, RANK), F32),
             pltpu.VMEM((1, TOKP), jnp.int32),
-            pltpu.VMEM((2, 8, 64, RANK), F32),
-            pltpu.VMEM((2, 8, 64, RANK), BF),
+            pltpu.VMEM((2, 128, TOKP), F32),
+            pltpu.VMEM((8, 64, RANK), F32),
+            pltpu.VMEM((8, 64, RANK), BF),
             pltpu.VMEM((8, 64, RANK), BF),
             pltpu.VMEM((8, 64, RANK), BF),
             pltpu.VMEM((8, 64, RANK), BF),
             pltpu.VMEM((16, 64, RANK), BF),
             pltpu.VMEM((2, 1024, 128), F32),
-            pltpu.VMEM((128, 128), F32),
-            pltpu.VMEM((16, 8, 128), F32),
+            pltpu.VMEM((2, 8, 8, 128), F32),
+            pltpu.VMEM((8, 8, 128), F32),
+            pltpu.VMEM((8, 8, 128), F32),
+            pltpu.VMEM((8, 8, 128), F32),
             dma((8,)),
             dma((4,)),
             dma,
@@ -446,8 +468,10 @@
             dma((4,)),
             dma((16,)),
             dma((16,)),
-            dma((16,)),
-            dma((16,)),
+            dma,
+            dma,
+            dma((8,)),
+            dma((8,)),
         ],
         compiler_params=pltpu.CompilerParams(
             collective_id=0, has_side_effects=True, vmem_limit_bytes=60 * 1024 * 1024
@@ -456,7 +480,7 @@
             flops=2 * 1460000000, bytes_accessed=12 * 1024 * 1024, transcendentals=0
         ),
     )(
-        ids,
+        turn_ids,
         turn_counts,
         activations,
         output_grads,

time: 76.8 us -> 74.5 us (0.970)
  local copies, waits for them, and re-layouts: 2.52 us -> 1.28 us
  Pallas kernels: 74.1 us -> 73.1 us
    reshape x1 -> x0, local copies, waits for them, and re-layouts: 1.24 us -> none  [local(): ids = turn_ids.reshape(1, TOK)]
    pallas_call x1, Pallas kernels: 74.1 us -> 73.1 us  [local(): pl.pallas_call(kernel, out_shape=jax.ShapeDtypeStruct((8, 64), F32), in_s...]
where the time goes in v3:
time: 74.5 us; the launch traced here: 74.3 us
  Pallas kernels  73.1 us (98%)
  local copies, waits for them, and re-layouts  1.28 us (2%)
    pallas_call x1, Pallas kernels, local(): pl.pallas_call(kernel, out_shape=jax.ShapeDtypeStruct((8, 64), F32), in_s...  73.1 us

profile of v3, /device:TPU:1, one launch (start us, length us, event | category | flops | bytes accessed | tf_op | source)
XLA Modules:
  0.0 74.3 jit_solution(1524744695356874044)
XLA Ops:
  0.0 73.1 %shard_map.73 = f32[8,64]{1,0:T(8,128)} custom-call(s32[320]{0:T(512)} %ids_ref.1, s32[4]{0:T(128)} %cnt_ref.1, bf16[320,8192]{1,0:T(8,128)(2,1)} %act_hbm.1, bf16[320,8192]{1,0:T(8,128)(2,1)} %og_hbm.1, bf16[512,256]{1,0:T(8,128)(2,1)} %ib_hbm.1, bf16[512,256]{1,0:T(8,128)(2,1)} %ob_hbm.1, bf16[128,4096]{1,0:T(8,128)(2,1)} %sg_hbm.1), custom_call_target="tpu_custom_call" | custom-call | flops 2920000000 | bytes 12582912 | tf_op jit(solution)/shard_map/pallas_call | solution.py:425
  73.1 1.3 %copy.9 = f32[64,8]{0,1:T(8,128)} copy(f32[64,8]{0,1:T(8,128)} %bitcast.1) | data formatting | bytes 4096

commit v4 on v3

--- a/solution.py
+++ b/solution.py
@@ -90,8 +90,9 @@
         return ((x * 4 + zz % 4), tok_of(y, zz // 4, c))
 
     sib = (T, K + 1 - 2 * c)
-    xdev = lambda d: (((x + d + 4) % 4) * 4 + zl, K)
-    ydev = lambda d: (T, tok_of((y + d + 4) % 4, h, c))
+    xs = {d: (((x + d + 4) % 4) * 4 + zl, K) for d in (1, -1)}
+    ys = {d: (T, tok_of((y + d + 4) % 4, h, c)) for d in (1, -1)}
+    me = y * 2 + h
     pair = (x * 4 + zl + 1 - 2 * (zl % 2), K)
     up = jnp.where(zl >= 2, 1, 7)
     over1 = zdev((z + up) % 8)
@@ -112,11 +113,15 @@
                     hbm.at[pl.ds(i * RB, RB)], A.at[b, pl.ds(i * RB, RB)], s_act.at[b * 4 + i]
                 )
             )
+    halves = (p, 1 - p)
     own = []
     for b, hbm in enumerate((ib_hbm, ob_hbm)):
-        for f in range(2):
+        for half in range(2):
+            rows = pl.ds(pl.multiple_of(halves[half] * PC, PC), PC)
             own.append(
-                pltpu.make_async_copy(hbm.at[pl.ds(f * PC, PC)], B.at[b, K, f], s_own.at[b * 2 + f])
+                pltpu.make_async_copy(
+                    hbm.at[rows], B.at[0, b, 0, 0, half], s_own.at[b * 2 + half]
+                )
             )
     stored = pltpu.make_async_copy(sg_hbm, S, s_sg)
     for cp in own:
@@ -127,18 +132,16 @@
 
     barrier = pltpu.get_barrier_semaphore()
 
-    def greet(i, _):
-        pl.semaphore_signal(
-            barrier, inc=1, device_id=(T, (K + i) % 16), device_id_type=MESH
-        )
-        pl.semaphore_signal(
-            barrier, inc=1, device_id=((T + i) % 16, K), device_id_type=MESH
-        )
-        return 0
-
-    lax.fori_loop(1, 16, greet, 0)
-
-    pl.semaphore_signal(barrier, inc=1, device_id=over2, device_id_type=MESH)
+    def greet(dev):
+        pl.semaphore_signal(barrier, inc=1, device_id=dev, device_id_type=MESH)
+
+    greet(sib)
+    greet(over2)
+    for i in range(1, 4):
+        greet((((x + i) % 4) * 4 + zl, K))
+        greet((x * 4 + (zl + i) % 4, K))
+    for i in range(1, 8):
+        greet((T, ((me + i) % 8) * 2 + c))
 
     @pl.when(edge)
     def _():
@@ -153,127 +156,133 @@
 
     @pl.when(edge)
     def _():
-        pl.semaphore_wait(barrier, 32)
+        pl.semaphore_wait(barrier, 16)
 
     @pl.when(jnp.logical_not(edge))
     def _():
-        pl.semaphore_wait(barrier, 31)
-
-    def part(b, kk, f, i):
-        return B.at[b, kk, f, pl.ds(i * R, R)], r_piece.at[((b * 16 + kk) * 2 + f) * NS + i]
+        pl.semaphore_wait(barrier, 15)
+
+    def part(key, i):
+        b, dy, dh, half = key
+        code = (((b * 4 + dy) * 2 + dh) * 2 + half) * NS + i
+        return B.at[0, b, dy, dh, half, pl.ds(i * R, R)], r_piece.at[code]
 
     sent = []
 
-    def send(b, kk, f, i, dev):
-        ref, rs = part(b, kk, f, i)
-        cp = rcopy(ref, ref, s_fwd.at[len(sent)], rs, dev)
+    def hand_on(key, i, dev, there):
+        cp = rcopy(part(key, i)[0], part(there, i)[0], s_fwd.at[len(sent)], part(there, i)[1], dev)
         cp.start()
         sent.append(cp)
 
-    for b in range(2):
-        for i in range(NS):
-            send(b, K, p, i, ydev(1))
-            send(b, K, p, i, ydev(-1))
+    def to_y(key, i, d):
+        b, dy, dh, half = key
+        hand_on(key, i, ys[d], (b, (dy - d) % 4, dh, half))
+
+    def to_x(key, i, d):
+        b, dy, dh, half = key
+        hand_on(key, i, xs[d], (b, dy, dh, 1 - half))
+
+    def to_pair(key, i):
+        b, dy, dh, half = key
+        hand_on(key, i, pair, (b, dy, dh, 1 - half))
 
     def boundary():
         out = []
         for b in range(2):
             for i in range(NS):
-                for far, (dev, f) in enumerate(((over1, p), (over2, 1 - p))):
-                    ref, rs = part(b, K, f, i)
-                    out.append(rcopy(ref, ref, s_out.at[(b * NS + i) * 2 + far], rs, dev))
+                for far, dev in enumerate((over1, over2)):
+                    ref, rs = part((b, 0, 1, 0), i)
+                    src = part((b, 0, 0, far), i)[0]
+                    out.append(rcopy(src, ref, s_out.at[(b * NS + i) * 2 + far], rs, dev))
         return out
 
-    @pl.when(edge)
-    def _():
-        for cp in boundary():
-            cp.start()
+    for b in range(2):
+        for i in range(NS):
+            to_y((b, 0, 0, 0), i, 1)
+            to_y((b, 0, 0, 0), i, -1)
+            if b == 0 and i == 0:
+
+                @pl.when(edge)
+                def _():
+                    for cp in boundary():
+                        cp.start()
 
     shared = []
 
-    def share(b, kk, f):
-        ref = B.at[b, kk] if f is None else B.at[b, kk, f]
-        rs = r_sib.at[(b * 16 + kk) * 2 + (0 if f is None else f)]
-        cp = rcopy(ref, ref, s_sib.at[len(shared)], rs, sib)
+    def share_copy(key, n):
+        b, dy, dh, half = key
+        at = (b, dy, dh) if half is None else (b, dy, dh, half)
+        rs = r_sib.at[((b * 4 + dy) * 2 + dh) * 2 + (half or 0)]
+        return rcopy(B.at[(0,) + at], B.at[(1,) + at], s_sib.at[n], rs, sib)
+
+    def share(key):
+        cp = share_copy(key, len(shared))
         cp.start()
         shared.append(cp)
 
-    def share_wait(b, kk, f):
-        ref = B.at[b, kk] if f is None else B.at[b, kk, f]
-        rs = r_sib.at[(b * 16 + kk) * 2 + (0 if f is None else f)]
-        rcopy(ref, ref, s_sib.at[0], rs, sib).wait_recv()
-
     for b in range(2):
-        share(b, K, None)
-    KO = K + 1 - 2 * c
-
-    def place(dy, dh, half):
-        hh = h if dh == 0 else 1 - h
-        return tok_of((y + dy) % 4, hh, c), (p if half == 0 else 1 - p)
+        share((b, 0, 0, None))
+
+    chunk = {
+        (dy, dh): tok_of((y + dy) % 4, h if dh == 0 else 1 - h, 0) for dy in range(4) for dh in range(2)
+    }
 
     def dots(b, blocks):
         lhs, rhs = [], []
-        for kk, f in blocks:
-            col = pl.multiple_of(kk * CH + f * PC, PC)
+        for core, dy, dh, half in blocks:
+            kk = chunk[dy, dh] + (c if core == 0 else 1 - c)
+            col = pl.multiple_of(kk * CH + halves[half] * PC, PC)
             lhs.append(A[b, :, pl.ds(col, PC)])
-            rhs.append(B[b, kk, f])
+            rhs.append(B[core, b, dy, dh, half])
         acc[b, pl.ds(0, TOK)] += jnp.dot(
             jnp.concatenate(lhs, axis=1), jnp.concatenate(rhs, axis=0), preferred_element_type=F32
         )
 
     def dots_of(b, group):
         if group == 0:
-            if b == 0:
-                for cp in loads[:4]:
-                    cp.wait()
-            else:
-                for cp in loads[4:]:
-                    cp.wait()
-            share_wait(b, KO, None)
-            dots(b, [(K, 0), (K, 1), (KO, 0), (KO, 1)])
+            for cp in loads[4 * b : 4 * b + 4]:
+                cp.wait()
+            share_copy((b, 0, 0, None), 0).wait_recv()
+            dots(b, [(core, 0, 0, half) for core in range(2) for half in range(2)])
             return
-        blocks = [place(*q) for q in HALVES[2 * group - 2 : 2 * group]]
-        others = [(kk + 1 - 2 * c, f) for kk, f in blocks]
+        keys = HALVES[2 * group - 2 : 2 * group]
+        blocks = [(0,) + q for q in keys]
         if group == 7:
             dots(b, blocks)
             blocks = []
-        for ko, f in others:
-            share_wait(b, ko, f)
-        dots(b, blocks + others)
-
-    seen = [{}, {}]
-    for n, code in enumerate(ORDER):
+        for q in keys:
+            share_copy((b,) + q, 0).wait_recv()
+        dots(b, blocks + [(1,) + q for q in keys])
+
+    events = []
+    for code in ORDER:
         i, half, dh, dy, b = code % NS, code // NS % 2, code // NS // 2 % 2, code // NS // 4 % 4, code // NS // 16
-        seen[b][(dy, dh, half)] = n
+        events.append(((b, dy, dh, half), i))
+    last = {key: n for n, (key, i) in enumerate(events)}
     due = []
     for b in range(2):
         due.append((NS + NS * b, b, 0))
         for group in range(1, 8):
-            last = max(seen[b][q] for q in HALVES[2 * group - 2 : 2 * group])
-            due.append((last + LAG, b, group))
+            n = max(last[(b,) + q] for q in HALVES[2 * group - 2 : 2 * group])
+            due.append((n + LAG, b, group))
     due.sort(key=lambda e: (e[0], e[2]))
 
-    parts = {}
-    for n, code in enumerate(ORDER):
-        i, half, dh, dy, b = code % NS, code // NS % 2, code // NS // 2 % 2, code // NS // 4 % 4, code // NS // 16
-        kk, f = place(dy, dh, half)
-        ref, rs = part(b, kk, f, i)
+    for n, (key, i) in enumerate(events):
+        b, dy, dh, half = key
+        ref, rs = part(key, i)
         rcopy(ref, ref, s_fwd.at[0], rs, sib).wait_recv()
-        if dy == 0:
-            if half == 0:
-                send(b, kk, f, i, ydev(1))
-                send(b, kk, f, i, ydev(-1))
-                send(b, kk, f, i, pair)
+        if half == 0 and dy == 0:
+            to_y(key, i, 1)
+            to_y(key, i, -1)
+            to_pair(key, i)
         elif half == 0:
             side = {3: 0, 1: 1, 2: b if dh == 0 else 1 - b}[dy]
             d = 1 if side == 0 else -1
             if dy != 2 and (b == side) == (dh == 0):
-                send(b, kk, f, i, ydev(d))
-            send(b, kk, f, i, xdev(d))
-        got = parts.setdefault((b, dy, dh, half), set())
-        got.add(i)
-        if len(got) == NS:
-            share(b, kk, f)
+                to_y(key, i, d)
+            to_x(key, i, d)
+        if last[key] == n:
+            share(key)
         while due and due[0][0] <= n:
             _, bb, group = due.pop(0)
             dots_of(bb, group)
@@ -297,7 +306,6 @@
     for t in range(TURN_G):
         Gf[:, pl.ds(t * 16, 16), :] = gradient(c, t)
     hc.wait_recv()
-    me = y * 2 + h
 
     def peer(i, sign):
         far = i < 4
@@ -437,7 +445,7 @@
         out_specs=pl.BlockSpec(memory_space=pltpu.VMEM),
         scratch_shapes=[
             pltpu.VMEM((2, TOK, D), BF),
-            pltpu.VMEM((2, 16, 2, PC, RANK), BF),
+            pltpu.VMEM((2, 2, 4, 2, 2, PC, RANK), BF),
             pltpu.VMEM((128, 4096), BF),
             pltpu.VMEM((2, TOKP, RANK), F32),
             pltpu.VMEM((1, TOKP), jnp.int32),
@@ -456,8 +464,8 @@
             dma((8,)),
             dma((4,)),
             dma,
-            dma((64 * NS,)),
-            dma((64,)),
+            dma((32 * NS,)),
+            dma((32,)),
             dma((32,)),
             dma((SEND_MAX,)),
             dma((4 * NS,)),

time: 74.5 us -> 73.3 us (0.984)
  Pallas kernels: 73.1 us -> 71.8 us
    pallas_call x1, Pallas kernels: 73.1 us -> 71.8 us  [local(): pl.pallas_call(kernel, out_shape=jax.ShapeDtypeStruct((8, 64), F32), in_s...]
where the time goes in v4:
time: 73.3 us; the launch traced here: 73.1 us
  Pallas kernels  71.8 us (98%)
  local copies, waits for them, and re-layouts  1.28 us (2%)
    pallas_call x1, Pallas kernels, local(): pl.pallas_call(kernel, out_shape=jax.ShapeDtypeStruct((8, 64), F32), in_s...  71.8 us

profile of v4, /device:TPU:1, one launch (start us, length us, event | category | flops | bytes accessed | tf_op | source)
XLA Modules:
  0.0 73.1 jit_solution(755048765446412211)
XLA Ops:
  0.0 71.8 %shard_map.73 = f32[8,64]{1,0:T(8,128)} custom-call(s32[320]{0:T(512)} %ids_ref.1, s32[4]{0:T(128)} %cnt_ref.1, bf16[320,8192]{1,0:T(8,128)(2,1)} %act_hbm.1, bf16[320,8192]{1,0:T(8,128)(2,1)} %og_hbm.1, bf16[512,256]{1,0:T(8,128)(2,1)} %ib_hbm.1, bf16[512,256]{1,0:T(8,128)(2,1)} %ob_hbm.1, bf16[128,4096]{1,0:T(8,128)(2,1)} %sg_hbm.1), custom_call_target="tpu_custom_call" | custom-call | flops 2920000000 | bytes 12582912 | tf_op jit(solution)/shard_map/pallas_call | solution.py:433
  71.9 1.3 %copy.9 = f32[64,8]{0,1:T(8,128)} copy(f32[64,8]{0,1:T(8,128)} %bitcast.1) | data formatting | bytes 4096

commit v5 on v4

--- a/solution.py
+++ b/solution.py
@@ -21,9 +21,9 @@
     45, 53, 58, 46, 63, 15, 23, 6, 62, 19, 39, 42, 22, 54, 7, 38,
     11, 30, 51, 59, 31, 18, 47, 55,
 )
-HALVES = ((1, 0, 0), (3, 0, 0), (0, 1, 0), (2, 0, 0), (3, 1, 0), (1, 1, 0), (2, 1, 0), (0, 1, 1), (1, 0, 1), (3, 0, 1), (3, 1, 1), (2, 0, 1), (1, 1, 1), (2, 1, 1))
 SEND_MAX = 4 * NS + 4 * NS + len(ORDER) * 2
-LAG = 3
+LAG = 13
+FIRST = 16
 BF = jnp.bfloat16
 F32 = jnp.float32
 MESH = pl.DeviceIdType.MESH
@@ -245,7 +245,7 @@
             share_copy((b, 0, 0, None), 0).wait_recv()
             dots(b, [(core, 0, 0, half) for core in range(2) for half in range(2)])
             return
-        keys = HALVES[2 * group - 2 : 2 * group]
+        keys = done[b][2 * group - 2 : 2 * group]
         blocks = [(0,) + q for q in keys]
         if group == 7:
             dots(b, blocks)
@@ -259,12 +259,13 @@
         i, half, dh, dy, b = code % NS, code // NS % 2, code // NS // 2 % 2, code // NS // 4 % 4, code // NS // 16
         events.append(((b, dy, dh, half), i))
     last = {key: n for n, (key, i) in enumerate(events)}
+    done = [sorted((k[1:] for k in last if k[0] == b), key=lambda q: last[(b,) + q]) for b in range(2)]
     due = []
     for b in range(2):
-        due.append((NS + NS * b, b, 0))
+        due.append((FIRST, b, 0))
         for group in range(1, 8):
-            n = max(last[(b,) + q] for q in HALVES[2 * group - 2 : 2 * group])
-            due.append((n + LAG, b, group))
+            n = max(last[(b,) + q] for q in done[b][2 * group - 2 : 2 * group])
+            due.append((max(n + LAG, FIRST), b, group))
     due.sort(key=lambda e: (e[0], e[2]))
 
     for n, (key, i) in enumerate(events):
@@ -283,7 +284,7 @@
             to_x(key, i, d)
         if last[key] == n:
             share(key)
-        while due and due[0][0] <= n:
+        if due and due[0][0] <= n:
             _, bb, group = due.pop(0)
             dots_of(bb, group)
     for _, bb, group in due:

time: 73.3 us -> 71.5 us (0.975)
  Pallas kernels: 71.8 us -> 70.1 us
    pallas_call x1, Pallas kernels: 71.8 us -> 70.1 us  [local(): pl.pallas_call(kernel, out_shape=jax.ShapeDtypeStruct((8, 64), F32), in_s...]
where the time goes in v5:
time: 71.5 us; the launch traced here: 71.4 us
  Pallas kernels  70.1 us (98%)
  local copies, waits for them, and re-layouts  1.28 us (2%)
    pallas_call x1, Pallas kernels, local(): pl.pallas_call(kernel, out_shape=jax.ShapeDtypeStruct((8, 64), F32), in_s...  70.1 us

profile of v5, /device:TPU:1, one launch (start us, length us, event | category | flops | bytes accessed | tf_op | source)
XLA Modules:
  0.0 71.4 jit_solution(8157477113408047322)
XLA Ops:
  0.0 70.1 %shard_map.73 = f32[8,64]{1,0:T(8,128)} custom-call(s32[320]{0:T(512)} %ids_ref.1, s32[4]{0:T(128)} %cnt_ref.1, bf16[320,8192]{1,0:T(8,128)(2,1)} %act_hbm.1, bf16[320,8192]{1,0:T(8,128)(2,1)} %og_hbm.1, bf16[512,256]{1,0:T(8,128)(2,1)} %ib_hbm.1, bf16[512,256]{1,0:T(8,128)(2,1)} %ob_hbm.1, bf16[128,4096]{1,0:T(8,128)(2,1)} %sg_hbm.1), custom_call_target="tpu_custom_call" | custom-call | flops 2920000000 | bytes 12582912 | tf_op jit(solution)/shard_map/pallas_call | solution.py:434
  70.1 1.3 %copy.9 = f32[64,8]{0,1:T(8,128)} copy(f32[64,8]{0,1:T(8,128)} %bitcast.1) | data formatting | bytes 4096

commit v6 on v5

--- a/solution.py
+++ b/solution.py
@@ -14,16 +14,14 @@
 RANK = 256
 CH = 512
 PC = 256
-NS = 2
+NS = 1
 ORDER = (
-    8, 24, 9, 25, 4, 40, 56, 5, 10, 41, 57, 16, 12, 17, 26, 48,
-    36, 28, 13, 37, 14, 49, 29, 60, 20, 61, 44, 50, 21, 27, 43, 52,
-    45, 53, 58, 46, 63, 15, 23, 6, 62, 19, 39, 42, 22, 54, 7, 38,
-    11, 30, 51, 59, 31, 18, 47, 55,
+    4, 12, 2, 28, 20, 8, 6, 18, 24, 3, 14, 30, 10, 22, 13, 29,
+    21, 19, 26, 5, 25, 9, 15, 7, 31, 11, 23, 27,
 )
 SEND_MAX = 4 * NS + 4 * NS + len(ORDER) * 2
-LAG = 13
-FIRST = 16
+LAG = 7
+FIRST = 8
 BF = jnp.bfloat16
 F32 = jnp.float32
 MESH = pl.DeviceIdType.MESH

time: 71.5 us -> 71.3 us (level)
  no operation moved by 1% of the time
where the time goes in v6:
time: 71.3 us; the launch traced here: 71.2 us
  Pallas kernels  69.9 us (98%)
  local copies, waits for them, and re-layouts  1.28 us (2%)
    pallas_call x1, Pallas kernels, local(): pl.pallas_call(kernel, out_shape=jax.ShapeDtypeStruct((8, 64), F32), in_s...  69.9 us

profile of v6, /device:TPU:1, one launch (start us, length us, event | category | flops | bytes accessed | tf_op | source)
XLA Modules:
  0.0 71.2 jit_solution(1464681632928052751)
XLA Ops:
  0.0 69.9 %shard_map.73 = f32[8,64]{1,0:T(8,128)} custom-call(s32[320]{0:T(512)} %ids_ref.1, s32[4]{0:T(128)} %cnt_ref.1, bf16[320,8192]{1,0:T(8,128)(2,1)} %act_hbm.1, bf16[320,8192]{1,0:T(8,128)(2,1)} %og_hbm.1, bf16[512,256]{1,0:T(8,128)(2,1)} %ib_hbm.1, bf16[512,256]{1,0:T(8,128)(2,1)} %ob_hbm.1, bf16[128,4096]{1,0:T(8,128)(2,1)} %sg_hbm.1), custom_call_target="tpu_custom_call" | custom-call | flops 2920000000 | bytes 12582912 | tf_op jit(solution)/shard_map/pallas_call | solution.py:432
  69.9 1.3 %copy.9 = f32[64,8]{0,1:T(8,128)} copy(f32[64,8]{0,1:T(8,128)} %bitcast.1) | data formatting | bytes 4096
